TPU v7x, 256 devices: a whole 4x4x8 slice. The times are simulated.
256 devices in a mesh: vocab: 16 (over z_lo, y, core), units: 16 (over x, z_hi).
Axes of the slice: x: 4, y: 4, z: 8 (z_hi: 4, z_lo: 2; z = z_hi * 2 + z_lo), core: 2. Of those that a mesh axis runs over, the one named last changes fastest.
Arguments:
- x_rows: bfloat16 [16, 16, 32, 1024], P('vocab', 'units'), may hold values from -16 to 16
- gain_in: float32 [1024], replicated, may hold values from 0.1 to 1.9
- w_in: bfloat16 [1024, 32768], P(None, 'units'), may hold values from -0.1875 to 0.1875
- w_out: bfloat16 [32768, 1024], P('units'), may hold values from -0.03125 to 0.03125
- gain_out: float32 [1024], replicated, may hold values from 0.1 to 1.9
- embed: bfloat16 [32256, 1024], P('vocab'), may hold values from -600 to 600
- targets: int32 [16, 16, 32], P(None, 'units'), may hold values from 0 to 32127
- row_mask: int32 [16, 16, 32], P(None, 'units'), may hold values 0 or 1
Outputs:
- grad_x: float32 [16, 16, 32, 1024], P('vocab', 'units')
Inputs may be any that keep to these rules, and one draw needn't show every extreme that they name: `targets`: ids of live vocabulary entries.
All inputs are finite; a program needn't handle non-finite values. No bound on the sum of `row_mask` on one device may be relied on, other than what follows from the above.
Results may differ from a plain program's by a relative error of at most 0.02.
The roundings to bfloat16 on the way count: a program that leaves them out, or rounds other values in their place, can miss the bound.
Values may be sent and summed in bfloat16 or wider, within the bound.
A program may use at most 64 MiB of HBM per device.

v0:
```python
import math

import jax
import jax.numpy as jnp
from jax import lax
from jax.sharding import PartitionSpec as P

D = 1024
VOCAB = 32128


EPSILON = 1e-06


def norm_scale(values):
    return lax.rsqrt(jnp.mean(values * values, axis=-1, keepdims=True) + EPSILON)


def norm_back(grad_in, values, scale_rows, gain_vec):
    scaled = grad_in * gain_vec
    inner_sum = jnp.mean(scaled * values, axis=-1, keepdims=True)
    return scaled * scale_rows - values * (scale_rows * scale_rows * scale_rows) * inner_sum


def contract_last(left, right):
    return lax.dot_general(
        left, right, (((1,), (1,)), ((), ())), preferred_element_type=jnp.float32
    )


def local(x_rows, gain_in, w_in, w_out, gain_out, embed, targets, row_mask):
    block_rows = x_rows.shape[2]
    model_width = x_rows.shape[3]
    unit_index = lax.axis_index("units")
    vocab_index = lax.axis_index("vocab")
    local_vocab = embed.shape[0]
    factor = 1.0 / math.sqrt(D)
    inputs = x_rows.reshape(block_rows, model_width).astype(jnp.float32)
    scale_in = norm_scale(inputs)
    normed = (inputs * scale_in * gain_in).astype(jnp.bfloat16)
    gathered = lax.all_gather(normed, "units", axis=0, tiled=True)
    before = jnp.dot(gathered, w_in, preferred_element_type=jnp.float32)
    active = jnp.maximum(before, 0.0).astype(jnp.bfloat16)
    totals = lax.psum(jnp.dot(active, w_out, preferred_element_type=jnp.float32), "units")
    branch_out = lax.dynamic_slice_in_dim(totals, unit_index * block_rows, block_rows, 0)
    summed = inputs + branch_out
    scale_out = norm_scale(summed)
    final_rows = (summed * scale_out * gain_out).astype(jnp.bfloat16)
    logits = contract_last(lax.all_gather(final_rows, "vocab", axis=0, tiled=True), embed) * factor
    columns = vocab_index * local_vocab + lax.broadcasted_iota(jnp.int32, (1, local_vocab), 1)
    live_cols = columns < VOCAB
    logits = jnp.where(live_cols, logits, -1e30)
    local_top = jnp.max(logits, axis=1)
    row_top = lax.pmax(local_top, "vocab")
    shifted = jnp.exp(logits - row_top[:, None])
    row_sum = lax.psum(jnp.sum(shifted, axis=1), "vocab")
    probability = shifted / row_sum[:, None]
    labels = targets.reshape(-1)
    weights = row_mask.reshape(-1).astype(jnp.float32)
    onehot = (columns == labels[:, None]).astype(jnp.float32)
    grad_logits = (weights[:, None] * (probability - onehot)).astype(jnp.bfloat16)
    grad_all = lax.psum(
        jnp.dot(grad_logits, embed, preferred_element_type=jnp.float32) * factor, "vocab"
    )
    grad_final = lax.dynamic_slice_in_dim(grad_all, vocab_index * block_rows, block_rows, 0)
    grad_sum = norm_back(grad_final, summed, scale_out, gain_out)
    grad_half = grad_sum.astype(jnp.bfloat16)
    product = contract_last(lax.all_gather(grad_half, "units", axis=0, tiled=True), w_out)
    grad_active = jnp.where(before > 0, product, 0.0).astype(jnp.bfloat16)
    grad_normed = lax.psum_scatter(
        contract_last(grad_active, w_in), "units", scatter_dimension=0, tiled=True
    )
    result = grad_sum + norm_back(grad_normed, inputs, scale_in, gain_in)
    return result.reshape(1, 1, block_rows, model_width)


def solution(mesh):
    in_specs = (
        P("vocab", "units", None, None),
        P(),
        P(None, "units"),
        P("units", None),
        P(),
        P("vocab", None),
        P(None, "units", None),
        P(None, "units", None),
    )
    out_specs = P("vocab", "units", None, None)
    return jax.shard_map(local, mesh=mesh, in_specs=in_specs, out_specs=out_specs, check_vma=False)
```

profile of v0, /device:TPU:8, one launch (start us, length us, event | category | flops | bytes accessed | tf_op | source)
XLA Modules:
  0.0 653.5 jit_solution(16331771151633158288)
XLA Ops:
  6.5 1.0 fusion.8
  7.5 1.6 fusion.10
  9.1 57.3 %all-gather.4.cloned.1.call-done = bf16[512,1024]{1,0:T(8,128)(2,1)} async-done(((bf16[32,1024]{1,0:T(8,128)(2,1)}), bf16[512,1024]{1,0:T(8,128)(2,1)}) %all-gather.4.cloned.1.call-update) | async-done | bytes 1048592 | tf_op jit(solution)/shard_map/all_gather | solution.py:41
  66.5 5.0 fusion.21
  71.5 1.9 copy-done.6
  73.4 3.7 fusion.2
  77.2 176.9 %all-reduce.3.cloned.1.call-done = f32[512,1024]{1,0:T(8,128)} async-done(((f32[512,1024]{1,0:T(8,128)}), f32[512,1024]{1,0:T(8,128)}) %all-reduce.3.cloned.1.call-update) | async-done | bytes 2097168 | tf_op jit(solution)/shard_map/psum | solution.py:44
  254.1 1.0 multiply_reduce_fusion.1
  255.2 1.6 multiply_convert_fusion.4
  257.4 0.6 reduce.7
  258.2 31.3 %all-gather.6.cloned.1.call-done = bf16[512,1024]{1,0:T(8,128)(2,1)} async-done(((bf16[32,1024]{1,0:T(8,128)(2,1)}), bf16[512,1024]{1,0:T(8,128)(2,1)}) %all-gather.6.cloned.1.call-update) | async-done | bytes 1048592 | tf_op jit(solution)/shard_map/all_gather | solution.py:49
  289.5 6.9 %fusion = (f32[512]{0:T(512)S(1)}, f32[512,2016]{0,1:T(8,128)}) fusion(pred[2016]{0:T(1024)(128)(4,1)S(1)} %broadcast_compare_fusion, bf16[512,1024]{1,0:T(8,128)(2,1)} %all-gather.6.cloned.1.call-done, bf16[2016,1024]{1,0:T(8,128)(2,1)} %param.13), kind=kOutput, calls=%fused_computation.5 | convolution fusion | flops 2117025280 | bytes 9310176 | tf_op jit(solution)/shard_map/dot_general | solution.py:26
  296.4 25.5 %pmax.7 = f32[512]{0:T(512)S(1)} all-reduce(f32[512]{0:T(512)S(1)} %get-tuple-element.9), channel_id=1, replica_groups=mesh['vocab'=16,'units'=16] {'vocab'}, use_global_device_ids=true, to_apply=%region_4.5 | all-reduce | flops 512 | bytes 4096 | tf_op jit(solution)/shard_map/pmax | solution.py:54
  321.9 2.9 fusion.1
  324.8 27.1 %psum.22 = f32[512]{0:T(512)S(1)} all-reduce(f32[512]{0:T(512)S(1)} %fusion.1), channel_id=1, replica_groups=mesh['vocab'=16,'units'=16] {'vocab'}, use_global_device_ids=true, to_apply=%region_6.7 | all-reduce | flops 512 | bytes 4096 | tf_op jit(solution)/shard_map/psum | solution.py:56
  351.9 7.4 %fusion.6 = f32[512,1024]{1,0:T(8,128)} fusion(bf16[2016,1024]{1,0:T(8,128)(2,1)} %param.13, f32[512,2016]{0,1:T(8,128)} %get-tuple-element.10, s32[512]{0:T(512)S(1)} %eq.16, f32[512]{0:T(512)S(1)} %psum.22, f32[512]{0:T(512)S(1)} %pmax.7, f32[512]{0:T(512)S(1)} %convert_element_type.38, s32[2016]{0:T(1024)S(1)} %iota_add_fusion, ...), kind=kOutput, calls=%fused_computation.11 | convolution fusion | flops 2123743232 | bytes 10372960 | tf_op jit(solution)/shard_map/dot_general | solution.py:63
  359.5 126.5 %all-reduce.5.cloned.1.call-done = f32[512,1024]{1,0:T(8,128)} async-done(((f32[512,1024]{1,0:T(8,128)}), f32[512,1024]{1,0:T(8,128)}) %all-reduce.5.cloned.1.call-update) | async-done | bytes 2097168 | tf_op jit(solution)/shard_map/psum | solution.py:62
  486.0 1.1 multiply_reduce_fusion
  487.1 1.7 fusion.20
  489.0 58.2 %all-gather.8.cloned.1.call-done = bf16[512,1024]{1,0:T(8,128)(2,1)} async-done(((bf16[32,1024]{1,0:T(8,128)(2,1)}), bf16[512,1024]{1,0:T(8,128)(2,1)}) %all-gather.8.cloned.1.call-update) | async-done | bytes 1048592 | tf_op jit(solution)/shard_map/all_gather | solution.py:68
  547.2 10.8 %fusion.7 = f32[512,1024]{1,0:T(8,128)} fusion(bf16[1024,2048]{1,0:T(8,128)(2,1)} %param.10, f32[512,2048]{1,0:T(8,128)} %copy-done.6, bf16[512,1024]{1,0:T(8,128)(2,1)} %all-gather.8.cloned.1.call-done, bf16[2048,1024]{1,0:T(8,128)(2,1)} %param.11), kind=kOutput, calls=%fused_computation.12 | convolution fusion | flops 4298113024 | bytes 15728640 | tf_op jit(solution)/shard_map/dot_general | solution.py:26
  558.0 85.8 %reduce-scatter.2.cloned.1.call-done = f32[32,1024]{1,0:T(8,128)} async-done(((f32[512,1024]{1,0:T(8,128)}), f32[32,1024]{1,0:T(8,128)}) %reduce-scatter.2.cloned.1.call-update) | async-done | bytes 131088 | tf_op jit(solution)/shard_map/reduce_scatter | solution.py:70
  643.8 1.0 fusion.15
  644.8 1.8 fusion.14
  (35 shorter events, 1.3 us)
Async XLA Ops:
  6.5 59.9 %all-gather.4.cloned.1.call-start = ((), (), s32[]{:S(2)}) async-start(), calls=%async_computation.1 | async-start | bytes 1114112 | tf_op jit(solution)/shard_map/all_gather | solution.py:41
  9.1 245.0 %all-reduce.3.cloned.1.call-start = ((), (), s32[]{:S(2)}) async-start(), calls=%async_computation.2 | async-start | bytes 4194304 | tf_op jit(solution)/shard_map/psum | solution.py:44
  66.5 6.9 %copy-start.5 = (bf16[2048,1024]{1,0:T(8,128)(2,1)S(1)}, bf16[2048,1024]{1,0:T(8,128)(2,1)}, u32[]{:S(2)}) copy-start(bf16[2048,1024]{1,0:T(8,128)(2,1)} %param.11) | copy-start | bytes 12582916
  71.4 1.9 copy-start.6
  73.4 180.7 %copy-start = (bf16[1,1,32,1024]{3,2,1,0:T(8,128)(2,1)S(1)}, bf16[1,1,32,1024]{3,2,1,0:T(8,128)(2,1)}, u32[]{:S(2)}) copy-start(bf16[1,1,32,1024]{3,2,1,0:T(8,128)(2,1)} %param.8) | copy-start | bytes 196612
  73.4 181.8 %copy-start.1 = (f32[1024]{0:T(1024)S(1)}, f32[1024]{0:T(1024)}, u32[]{:S(2)}) copy-start(f32[1024]{0:T(1024)} %param.12) | copy-start | bytes 12292
  73.4 184.0 %copy-start.3 = (s32[16,1,32]{2,1,0:T(1,128)S(1)}, s32[16,1,32]{2,1,0:T(1,128)}, u32[]{:S(2)}) copy-start(s32[16,1,32]{2,1,0:T(1,128)} %param.14) | copy-start | bytes 6148
  73.4 184.7 %copy-start.4 = (s32[16,1,32]{2,1,0:T(1,128)S(1)}, s32[16,1,32]{2,1,0:T(1,128)}, u32[]{:S(2)}) copy-start(s32[16,1,32]{2,1,0:T(1,128)} %param.15) | copy-start | bytes 6148
  77.1 212.4 %all-gather.6.cloned.1.call-start = ((), (), s32[]{:S(2)}) async-start(), calls=%async_computation.3 | async-start | bytes 1114112 | tf_op jit(solution)/shard_map/all_gather | solution.py:49
  256.8 229.2 %all-reduce.5.cloned.1.call-start = ((), (), s32[]{:S(2)}) async-start(), calls=%async_computation.4 | async-start | bytes 4194304 | tf_op jit(solution)/shard_map/psum | solution.py:62
  359.4 187.8 %all-gather.8.cloned.1.call-start = ((), (), s32[]{:S(2)}) async-start(), calls=%async_computation.5 | async-start | bytes 1114112 | tf_op jit(solution)/shard_map/all_gather | solution.py:68
  488.8 155.0 %copy-start.2 = (f32[1024]{0:T(1024)S(1)}, f32[1024]{0:T(1024)}, u32[]{:S(2)}) copy-start(f32[1024]{0:T(1024)} %param.9) | copy-start | bytes 12292
  488.8 155.0 %reduce-scatter.2.cloned.1.call-start = ((), (), s32[]{:S(2)}) async-start(), calls=%async_computation.6 | async-start | bytes 2228224 | tf_op jit(solution)/shard_map/reduce_scatter | solution.py:70
Sparse Core Ops, SparseCore 0:
  9.8 56.6 all-gather.3
  77.2 176.8 all-reduce.2
  256.9 32.5 all-gather.5
  359.5 126.3 all-reduce.4
  488.9 58.2 all-gather.7
  558.1 85.5 reduce-scatter.1
where the time goes:
time: 654 us; the launch traced here: 653 us
  waiting for transfers between devices  536 us (82%)
  blocking collectives  52.6 us (8%)
  matrix products  33.8 us (5%)
  other arithmetic  14.4 us (2%)
  between operations  13.6 us (2%)
    psum x1, waiting for transfers between devices, local(): lax.psum(jnp.dot(active, w_out, preferred_element_type=jnp.float32), 'uni...  177 us
    psum x1, waiting for transfers between devices, local(): lax.psum(jnp.dot(grad_logits, embed, preferred_element_type=jnp.float32)...  126 us
    reduce_scatter x1, waiting for transfers between devices, local(): lax.psum_scatter(contract_last(grad_active, w_in), 'units', scatter_dimen...  85.8 us
    all_gather x1, waiting for transfers between devices, local(): lax.all_gather(grad_half, 'units', axis=0, tiled=True)  58.2 us
    all_gather x1, waiting for transfers between devices, local(): gathered = lax.all_gather(normed, 'units', axis=0, tiled=True)  57.3 us
    all_gather x1, waiting for transfers between devices, local(): lax.all_gather(final_rows, 'vocab', axis=0, tiled=True)  31.3 us
    psum x1, blocking collectives, local(): row_sum = lax.psum(jnp.sum(shifted, axis=1), 'vocab')  27.1 us
    pmax x1, blocking collectives, local(): row_top = lax.pmax(local_top, 'vocab')  25.5 us
  transfers between devices with their start and end apart: 6, of which 6 were waited for; matrix products, arithmetic and copies ran while one was open for 0% of the time, Pallas kernels for 0%

commit v1 on v0

v1 whole, which is shorter than its diff:
```python
import functools
import math

import jax
import jax.numpy as jnp
from jax import lax
from jax.experimental import pallas as pl
from jax.experimental.pallas import tpu as pltpu
from jax.sharding import PartitionSpec as P

D = 1024
VOCAB = 32128
EPSILON = 1e-06
CHUNKS = 2
F32, BF16 = jnp.float32, jnp.bfloat16
MESH = pl.DeviceIdType.MESH
STEPS = (2, 1, 3)
CHIP_STEPS = ((1, 2), (0, 2), (1, 1), (1, 3), (0, 1), (0, 3), (1, 0))
PEER_STEPS = tuple(s + (c,) for s in CHIP_STEPS for c in (0, 1)) + ((0, 0, 1),)
NT = (((1,), (1,)), ((), ()))


def norm_scale(values):
    return lax.rsqrt(jnp.mean(values * values, axis=-1, keepdims=True) + EPSILON)


def norm_back(grad_in, values, scale_rows, gain_vec):
    scaled = grad_in * gain_vec
    inner_sum = jnp.mean(scaled * values, axis=-1, keepdims=True)
    return scaled * scale_rows - values * (scale_rows * scale_rows * scale_rows) * inner_sum


def eye(rows, columns, shift=0):
    row = lax.broadcasted_iota(jnp.int32, (rows, columns), 0)
    return row + shift == lax.broadcasted_iota(jnp.int32, (rows, columns), 1)


def as_row(column):
    return jnp.sum(jnp.where(eye(128, 128), column, 0.0), axis=0, keepdims=True)


def as_column(row, mask):
    return jnp.sum(jnp.where(mask, row, 0.0), axis=1, keepdims=True)


def kernel(
    x_ref, gain_in_ref, w_in_hbm, w_out_hbm, gain_out_ref, embed_hbm, targets_ref, mask_ref,
    out_ref,
    w_in, w_out, embed, near, active, logits, grads, label, weight,
    fwd_all, fwd_part, fwd_own, fwd_x, fwd_mid, fwd_z,
    head_all, stats, stats_in, head_part, head_core, head_mid, head_in,
    bwd_all, bwd_part, bwd_own, bwd_x, bwd_mid, bwd_z,
    summed_ref, grad_sum_ref, local_sem, send_sem, recv_sem,
):
    vocab = lax.axis_index("vocab")
    unit = lax.axis_index("units")
    x_at, z_at = unit // 4, unit % 4
    core, y_at, zlo_at = vocab % 2, (vocab // 2) % 4, vocab // 8
    local_vocab = embed_hbm.shape[0]
    padded_vocab = embed.shape[0]
    block = x_ref.shape[0]
    part = block // CHUNKS
    rows = 16 * part
    hidden = w_in.shape[1]
    factor = 1.0 / math.sqrt(D)
    chunks = range(CHUNKS)

    def unit_peer(dx, dz):
        return vocab, ((x_at + dx) % 4) * 4 + (z_at + dz) % 4

    def vocab_peer(dzlo, dy, dcore):
        return ((zlo_at + dzlo) % 2) * 8 + ((y_at + dy) % 4) * 2 + (core + dcore) % 2, unit

    def chip_slot(dzlo, dy):
        return ((zlo_at + dzlo) % 2) * 4 + (y_at + dy) % 4

    def take(start, size):
        return pl.ds(pl.multiple_of(start, size), size)

    used = [0]
    started = []

    def send(src, dst, peer):
        k = used[0]
        used[0] += 1
        copy = pltpu.make_async_remote_copy(
            src_ref=src, dst_ref=dst, send_sem=send_sem.at[k], recv_sem=recv_sem.at[k],
            device_id=peer, device_id_type=MESH,
        )
        copy.start()
        started.append(copy)
        return copy

    loads = [
        pltpu.make_async_copy(w_in_hbm, w_in, local_sem.at[0]),
        pltpu.make_async_copy(w_out_hbm, w_out, local_sem.at[1]),
        pltpu.make_async_copy(embed_hbm, embed.at[pl.ds(0, local_vocab)], local_sem.at[2]),
    ]
    for load in loads:
        load.start()

    barrier = pltpu.get_barrier_semaphore()
    greet = [unit_peer(d, 0) for d in STEPS] + [unit_peer(0, d) for d in STEPS]
    greet += [vocab_peer(*s) for s in PEER_STEPS]
    for peer in greet:
        pl.semaphore_signal(barrier, inc=1, device_id=peer, device_id_type=MESH)

    inputs = x_ref[...].astype(F32)
    scale_in = norm_scale(inputs)
    normed = (inputs * scale_in * gain_in_ref[...]).astype(BF16)
    for c in chunks:
        fwd_all[c, 0:part, :] = normed[c * part : (c + 1) * part]
    embed[local_vocab:, :] = jnp.zeros((padded_vocab - local_vocab, D), BF16)
    pl.semaphore_wait(barrier, len(greet))

    def unit_gather_start(buf):
        along_z = [
            send(buf.at[pl.ds(0, part)], buf.at[pl.ds((4 - d) * part, part)], unit_peer(0, d))
            for d in STEPS
        ]
        along_x = [
            send(buf.at[pl.ds(0, part)], buf.at[pl.ds((4 - d) * 4 * part, part)], unit_peer(d, 0))
            for d in STEPS
        ]
        return along_z, along_x

    def unit_gather_pass(buf, along_z, along_x):
        for copy in along_z:
            copy.wait_recv()
        return along_x + [
            send(
                buf.at[pl.ds(part, 3 * part)],
                buf.at[pl.ds(((4 - d) * 4 + 1) * part, 3 * part)],
                unit_peer(d, 0),
            )
            for d in STEPS
        ]

    def unit_sum_start(partial, landing):
        return [
            send(partial.at[pl.ds(d * 4 * part, 4 * part)], landing.at[d - 1], unit_peer(d, 0))
            for d in STEPS
        ]

    def unit_sum_pass(copies, own, landing, mid, landing_z):
        for copy in copies:
            copy.wait_recv()
        total = own[...]
        for d in (1, 2, 3):
            total = total + landing[d - 1].astype(F32)
        own[...] = total
        mid[...] = total.astype(BF16)
        return [
            send(mid.at[pl.ds(d * part, part)], landing_z.at[d - 1], unit_peer(0, d))
            for d in STEPS
        ]

    def unit_sum_end(copies, own, landing_z):
        for copy in copies:
            copy.wait_recv()
        total = own[0:part, :]
        for d in (1, 2, 3):
            total = total + landing_z[d - 1].astype(F32)
        return total

    fwd = [unit_gather_start(fwd_all.at[c]) for c in chunks]

    for c in chunks:
        pick = eye(part, block, c * part)
        for slot in range(16):
            owner = ((slot // 4) % 2) * 8 + (slot % 4) * 2 + slot // 8
            label[c, slot * part : (slot + 1) * part, :] = as_column(
                targets_ref[owner].astype(F32), pick
            )
            weight[c, slot * part : (slot + 1) * part, :] = as_column(
                mask_ref[owner].astype(F32), pick
            )

    fwd = [unit_gather_pass(fwd_all.at[c], *fwd[c]) for c in chunks]

    fwd_sum = []
    for c in chunks:
        if c == 0:
            loads[0].wait()
        for copy in fwd[c]:
            copy.wait_recv()

        @pl.loop(0, hidden // 512)
        def _(j):
            at = take(j * 512, 512)
            before = jnp.dot(fwd_all[c], w_in[:, at], preferred_element_type=F32)
            active[c, :, at] = jnp.maximum(before, 0.0).astype(BF16)

        if c == 0:
            loads[1].wait()

        @pl.loop(0, D // 512)
        def _(j):
            at = take(j * 512, 512)
            product = jnp.dot(active[c], w_out[:, at], preferred_element_type=F32)
            fwd_own[c, :, at] = product[0 : 4 * part]
            fwd_part[c, :, at] = product.astype(BF16)

        fwd_sum.append(unit_sum_start(fwd_part.at[c], fwd_x.at[c]))

    fwd_sum = [
        unit_sum_pass(fwd_sum[c], fwd_own.at[c], fwd_x.at[c], fwd_mid.at[c], fwd_z.at[c])
        for c in chunks
    ]

    my_slot = core * 8 + chip_slot(0, 0)
    head = []
    for c in chunks:
        summed = inputs[c * part : (c + 1) * part] + unit_sum_end(
            fwd_sum[c], fwd_own.at[c], fwd_z.at[c]
        )
        summed_ref[c] = summed
        final = (summed * norm_scale(summed) * gain_out_ref[...]).astype(BF16)
        mine = head_all.at[c, take(my_slot * part, part)]
        mine[...] = final
        head.append([send(mine, mine, vocab_peer(*s, 0)) for s in CHIP_STEPS])
        head[c].append(send(mine, mine, vocab_peer(0, 0, 1)))

    loads[2].wait()
    lane = lax.broadcasted_iota(jnp.int32, (1, 512), 1)
    exchange = []
    top = []
    for c in chunks:
        across = [head[c][-1]]
        for copy, (dzlo, dy) in reversed(list(zip(head[c][:-1], CHIP_STEPS))):
            copy.wait_recv()
            slot = head_all.at[c, take((core * 8 + chip_slot(-dzlo, -dy)) * part, part)]
            across.append(send(slot, slot, vocab_peer(0, 0, 1)))
        for copy in across:
            copy.wait_recv()

        def logits_tile(j, best):
            at = take(j * 512, 512)
            tile = lax.dot_general(head_all[c], embed[at, :], NT, preferred_element_type=F32)
            here = lane + j * 512
            live = jnp.logical_and(here < local_vocab, here + vocab * local_vocab < VOCAB)
            tile = jnp.where(live, tile * factor, -1e30)
            logits[c, :, at] = tile
            for k in range(4):
                best = jnp.maximum(best, tile[:, k * 128 : (k + 1) * 128])
            return best

        best = lax.fori_loop(
            0, padded_vocab // 512, logits_tile, jnp.full((rows, 128), -1e30, F32)
        )
        local_top = jnp.max(best, axis=1, keepdims=True)

        def exp_tile(j, acc):
            at = take(j * 512, 512)
            tile = jnp.exp(logits[c, :, at] - local_top)
            logits[c, :, at] = tile
            for k in range(4):
                acc = acc + tile[:, k * 128 : (k + 1) * 128]
            return acc

        acc = lax.fori_loop(0, padded_vocab // 512, exp_tile, jnp.zeros((rows, 128), F32))
        local_sum = jnp.sum(acc, axis=1, keepdims=True)
        halves = rows // 128
        stats[c] = jnp.zeros((8, 128), F32)
        for h in range(halves):
            stats[c, h : h + 1, :] = as_row(local_top[h * 128 : (h + 1) * 128])
            stats[c, 4 + h : 5 + h, :] = as_row(local_sum[h * 128 : (h + 1) * 128])
        exchange.append(
            [send(stats.at[c], stats_in.at[c, k], vocab_peer(*s)) for k, s in enumerate(PEER_STEPS)]
        )

    head_sum = []
    for c in chunks:
        for copy in exchange[c]:
            copy.wait_recv()
        own_top, own_sum = stats[c, 0:4, :], stats[c, 4:8, :]
        row_top = own_top
        for k in range(len(PEER_STEPS)):
            row_top = jnp.maximum(row_top, stats_in[c, k, 0:4, :])
        row_sum = own_sum * jnp.exp(own_top - row_top)
        for k in range(len(PEER_STEPS)):
            row_sum = row_sum + stats_in[c, k, 4:8, :] * jnp.exp(stats_in[c, k, 0:4, :] - row_top)
        ratio_rows = jnp.exp(own_top - row_top) / row_sum
        ratio = jnp.concatenate(
            [as_column(ratio_rows[h : h + 1], eye(128, 128)) for h in range(rows // 128)], axis=0
        )
        wanted = label[c].astype(jnp.int32) - vocab * local_vocab

        @pl.loop(0, padded_vocab // 512)
        def _(j):
            at = take(j * 512, 512)
            onehot = (lane + j * 512 == wanted).astype(F32)
            grads[c, :, at] = (weight[c] * (logits[c, :, at] * ratio - onehot)).astype(BF16)

        @pl.loop(0, D // 512)
        def _(j):
            at = take(j * 512, 512)
            product = jnp.dot(grads[c], embed[:, at], preferred_element_type=F32) * factor
            head_part[c, :, at] = product.astype(BF16)

        half = rows // 2
        head_sum.append(
            send(
                head_part.at[c, take((1 - core) * half, half)], head_core.at[c],
                vocab_peer(0, 0, 1),
            )
        )

    for c in chunks:
        head_sum[c].wait_recv()
        half = rows // 2
        total = head_part[c, take(core * half, half), :].astype(F32) + head_core[c].astype(F32)
        head_mid[c] = total.astype(BF16)
        head_sum[c] = [
            send(
                head_mid.at[c, take(chip_slot(*s) * part, part)], head_in.at[c, k],
                vocab_peer(*s, 0),
            )
            for k, s in enumerate(CHIP_STEPS)
        ]

    bwd = []
    for c in chunks:
        for copy in head_sum[c]:
            copy.wait_recv()
        grad_final = head_mid[c, take(chip_slot(0, 0) * part, part), :].astype(F32)
        for k in range(len(CHIP_STEPS)):
            grad_final = grad_final + head_in[c, k].astype(F32)
        summed = summed_ref[c]
        grad_sum = norm_back(grad_final, summed, norm_scale(summed), gain_out_ref[...])
        grad_sum_ref[c] = grad_sum
        bwd_all[c, 0:part, :] = grad_sum.astype(BF16)
        bwd.append(unit_gather_start(bwd_all.at[c]))
    bwd = [unit_gather_pass(bwd_all.at[c], *bwd[c]) for c in chunks]

    bwd_sum = []
    for c in chunks:
        for copy in bwd[c]:
            copy.wait_recv()

        @pl.loop(0, hidden // 512)
        def _(j):
            at = take(j * 512, 512)
            product = lax.dot_general(bwd_all[c], w_out[at, :], NT, preferred_element_type=F32)
            held = active[c, :, at]
            near[c, :, at] = jnp.where(held.astype(F32) > 0.0, product, 0.0).astype(BF16)

        @pl.loop(0, D // 512)
        def _(j):
            at = take(j * 512, 512)
            product = lax.dot_general(near[c], w_in[at, :], NT, preferred_element_type=F32)
            bwd_own[c, :, at] = product[0 : 4 * part]
            bwd_part[c, :, at] = product.astype(BF16)

        bwd_sum.append(unit_sum_start(bwd_part.at[c], bwd_x.at[c]))

    bwd_sum = [
        unit_sum_pass(bwd_sum[c], bwd_own.at[c], bwd_x.at[c], bwd_mid.at[c], bwd_z.at[c])
        for c in chunks
    ]
    for c in chunks:
        grad_normed = unit_sum_end(bwd_sum[c], bwd_own.at[c], bwd_z.at[c])
        here = slice(c * part, (c + 1) * part)
        out_ref[here, :] = grad_sum_ref[c] + norm_back(
            grad_normed, inputs[here], scale_in[here], gain_in_ref[...]
        )
    for copy in started:
        copy.wait_send()


def local(x_rows, gain_in, w_in, w_out, gain_out, embed, targets, row_mask):
    block = x_rows.shape[2]
    part = block // CHUNKS
    rows = 16 * part
    hidden = w_in.shape[1]
    padded_vocab = (embed.shape[0] + 511) // 512 * 512
    c = CHUNKS
    unit_sum = [
        pltpu.VMEM((c, rows, D), BF16),
        pltpu.VMEM((c, rows, D), BF16),
        pltpu.VMEM((c, 4 * part, D), F32),
        pltpu.VMEM((c, 3, 4 * part, D), BF16),
        pltpu.VMEM((c, 4 * part, D), BF16),
        pltpu.VMEM((c, 3, part, D), BF16),
    ]
    scratch = [
        pltpu.VMEM(w_in.shape, BF16),
        pltpu.VMEM(w_out.shape, BF16),
        pltpu.VMEM((padded_vocab, D), BF16),
        pltpu.VMEM((c, rows, hidden), BF16),
        pltpu.VMEM((c, rows, hidden), BF16),
        pltpu.VMEM((c, rows, padded_vocab), F32),
        pltpu.VMEM((c, rows, padded_vocab), BF16),
        pltpu.VMEM((c, rows, 1), F32),
        pltpu.VMEM((c, rows, 1), F32),
        *unit_sum,
        pltpu.VMEM((c, rows, D), BF16),
        pltpu.VMEM((c, 8, 128), F32),
        pltpu.VMEM((c, 15, 8, 128), F32),
        pltpu.VMEM((c, rows, D), BF16),
        pltpu.VMEM((c, rows // 2, D), BF16),
        pltpu.VMEM((c, rows // 2, D), BF16),
        pltpu.VMEM((c, 7, part, D), BF16),
        *unit_sum,
        pltpu.VMEM((c, part, D), F32),
        pltpu.VMEM((c, part, D), F32),
        pltpu.SemaphoreType.DMA((3,)),
        pltpu.SemaphoreType.DMA((160,)),
        pltpu.SemaphoreType.DMA((160,)),
    ]
    vmem = pl.BlockSpec(memory_space=pltpu.VMEM)
    anywhere = pl.BlockSpec(memory_space=pl.ANY)
    result = pl.pallas_call(
        kernel,
        out_shape=jax.ShapeDtypeStruct((block, D), F32),
        in_specs=[vmem, vmem, anywhere, anywhere, vmem, anywhere, vmem, vmem],
        out_specs=vmem,
        scratch_shapes=scratch,
        compiler_params=pltpu.CompilerParams(
            collective_id=0, has_side_effects=True, vmem_limit_bytes=56 * 1024 * 1024
        ),
        cost_estimate=pl.CostEstimate(
            flops=12 * 512 * D * hidden, bytes_accessed=6 * hidden * D, transcendentals=0
        ),
    )(
        x_rows.reshape(block, D), gain_in.reshape(1, D), w_in, w_out, gain_out.reshape(1, D), embed,
        targets, row_mask,
    )
    return result.reshape(1, 1, block, D)


def solution(mesh):
    in_specs = (
        P("vocab", "units", None, None),
        P(),
        P(None, "units"),
        P("units", None),
        P(),
        P("vocab", None),
        P(None, "units", None),
        P(None, "units", None),
    )
    out_specs = P("vocab", "units", None, None)
    return jax.shard_map(local, mesh=mesh, in_specs=in_specs, out_specs=out_specs, check_vma=False)
```

time: 654 us -> 105 us (0.16)
  waiting for transfers between devices: 536 us -> 0 us
  Pallas kernels: 0 us -> 102 us
  blocking collectives: 52.6 us -> 0 us
  matrix products: 33.8 us -> 0 us
  other arithmetic: 14.4 us -> 0 us
  between operations: 13.6 us -> 0.01 us
    psum x2 -> x0, waiting for transfers between devices: 303 us -> none  [the longest x1 177 us: local(): lax.psum(jnp.dot(active, w_out, preferred_element_type=jnp.float32), 'uni...]
    all_gather x3 -> x0, waiting for transfers between devices: 147 us -> none  [the longest x1 58.2 us: local(): lax.all_gather(grad_half, 'units', axis=0, tiled=True)]
    pallas_call x0 -> x1, Pallas kernels: none -> 102 us  [local(): pl.pallas_call(kernel, out_shape=jax.ShapeDtypeStruct((block, D), F32), i...]
    reduce_scatter x1 -> x0, waiting for transfers between devices: 85.8 us -> none  [local(): lax.psum_scatter(contract_last(grad_active, w_in), 'units', scatter_dimen...]
    dot_general x5 -> x0, matrix products: 33.8 us -> none  [the longest x2 17.7 us: contract_last(): lax.dot_general(left, right, (((1,), (1,)), ((), ())), preferred_element_...]
    psum x1 -> x0, blocking collectives: 27.1 us -> none  [local(): row_sum = lax.psum(jnp.sum(shifted, axis=1), 'vocab')]
    pmax x1 -> x0, blocking collectives: 25.5 us -> none  [local(): row_top = lax.pmax(local_top, 'vocab')]
    reduce_sum x5 -> x0, other arithmetic: 7.02 us -> none  [the longest x1 2.9 us: local(): row_sum = lax.psum(jnp.sum(shifted, axis=1), 'vocab')]
  transfers between devices with their start and end apart: 6 -> 0, of which waited for: 6 -> 0; matrix products, arithmetic and copies ran while one was open for 0% -> 0% of each run, Pallas kernels for 0% -> 0%
where the time goes in v1:
time: 105 us; the launch traced here: 103 us
  Pallas kernels  102 us (97%)
  local copies, waits for them, and re-layouts  1.57 us (1%)
    pallas_call x1, Pallas kernels, local(): pl.pallas_call(kernel, out_shape=jax.ShapeDtypeStruct((block, D), F32), i...  102 us

profile of v1, /device:TPU:8, one launch (start us, length us, event | category | flops | bytes accessed | tf_op | source)
XLA Modules:
  0.0 103.4 jit_solution(6318315268530751967)
XLA Ops:
  0.0 101.8 %shard_map.82 = f32[32,1024]{1,0:T(8,128)} custom-call(bf16[32,1024]{1,0:T(8,128)(2,1)} %bitcast.5, f32[1,1024]{1,0:T(1,128)} %bitcast.6, bf16[1024,2048]{1,0:T(8,128)(2,1)} %w_in_hbm.1, bf16[2048,1024]{1,0:T(8,128)(2,1)} %w_out_hbm.1, f32[1,1024]{1,0:T(1,128)} %bitcast.7, bf16[2016,1024]{1,0:T(8,128)(2,1)} %embed_hbm.1, s32[16,1,32]{2,1,0:T(1,128)} %targets_ref.1, ...), custom_call_target="tpu_custom_call" | custom-call | flops 12884901888 | bytes 12582912 | tf_op jit(solution)/shard_map/pallas_call | solution.py:413
  101.8 1.6 %copy.10 = f32[1,1,32,1024]{3,2,1,0:T(8,128)} copy(f32[1,1,32,1024]{3,2,1,0:T(8,128)} %bitcast.4) | data formatting | bytes 262144

commit v2 on v1

--- a/solution.py
+++ b/solution.py
@@ -12,6 +12,8 @@
 VOCAB = 32128
 EPSILON = 1e-06
 CHUNKS = 2
+TILE = 256
+SENDS = 99 * CHUNKS
 F32, BF16 = jnp.float32, jnp.bfloat16
 MESH = pl.DeviceIdType.MESH
 STEPS = (2, 1, 3)
@@ -74,6 +76,9 @@
     def chip_slot(dzlo, dy):
         return ((zlo_at + dzlo) % 2) * 4 + (y_at + dy) % 4
 
+    def tiles(size):
+        return [slice(start, start + TILE) for start in range(0, size, TILE)]
+
     def take(start, size):
         return pl.ds(pl.multiple_of(start, size), size)
 
@@ -124,36 +129,49 @@
         ]
         return along_z, along_x
 
-    def unit_gather_pass(buf, along_z, along_x):
-        for copy in along_z:
-            copy.wait_recv()
-        return along_x + [
-            send(
-                buf.at[pl.ds(part, 3 * part)],
-                buf.at[pl.ds(((4 - d) * 4 + 1) * part, 3 * part)],
-                unit_peer(d, 0),
-            )
-            for d in STEPS
-        ]
+    def unit_gather_pass(buf, along_z, along_x, which):
+        for k in which:
+            along_z[k].wait_recv()
+            dz = 4 - STEPS[k]
+            along_x += [
+                send(
+                    buf.at[pl.ds(dz * part, part)],
+                    buf.at[pl.ds(((4 - d) * 4 + dz) * part, part)],
+                    unit_peer(d, 0),
+                )
+                for d in STEPS
+            ]
 
     def unit_sum_start(partial, landing):
         return [
-            send(partial.at[pl.ds(d * 4 * part, 4 * part)], landing.at[d - 1], unit_peer(d, 0))
-            for d in STEPS
+            [
+                send(
+                    partial.at[pl.ds((d * 4 + dz) * part, part)],
+                    landing.at[d - 1, pl.ds(dz * part, part)],
+                    unit_peer(d, 0),
+                )
+                for d in STEPS
+            ]
+            for dz in STEPS + (0,)
         ]
 
     def unit_sum_pass(copies, own, landing, mid, landing_z):
-        for copy in copies:
-            copy.wait_recv()
-        total = own[...]
-        for d in (1, 2, 3):
-            total = total + landing[d - 1].astype(F32)
-        own[...] = total
-        mid[...] = total.astype(BF16)
-        return [
-            send(mid.at[pl.ds(d * part, part)], landing_z.at[d - 1], unit_peer(0, d))
-            for d in STEPS
-        ]
+        along_z = []
+        for dz, arrivals in zip(STEPS + (0,), copies):
+            for copy in arrivals:
+                copy.wait_recv()
+            at = slice(dz * part, (dz + 1) * part)
+            total = own[at, :]
+            for d in (1, 2, 3):
+                total = total + landing[d - 1, at, :].astype(F32)
+            if dz:
+                mid[at, :] = total.astype(BF16)
+                along_z.append(
+                    send(mid.at[pl.ds(dz * part, part)], landing_z.at[dz - 1], unit_peer(0, dz))
+                )
+            else:
+                own[at, :] = total
+        return along_z
 
     def unit_sum_end(copies, own, landing_z):
         for copy in copies:
@@ -176,27 +194,25 @@
                 mask_ref[owner].astype(F32), pick
             )
 
-    fwd = [unit_gather_pass(fwd_all.at[c], *fwd[c]) for c in chunks]
+    for which in ((1, 2), (0,)):
+        for c in chunks:
+            unit_gather_pass(fwd_all.at[c], *fwd[c], which)
 
     fwd_sum = []
     for c in chunks:
         if c == 0:
             loads[0].wait()
-        for copy in fwd[c]:
-            copy.wait_recv()
-
-        @pl.loop(0, hidden // 512)
-        def _(j):
-            at = take(j * 512, 512)
+        for copy in fwd[c][1]:
+            copy.wait_recv()
+
+        for at in tiles(hidden):
             before = jnp.dot(fwd_all[c], w_in[:, at], preferred_element_type=F32)
             active[c, :, at] = jnp.maximum(before, 0.0).astype(BF16)
 
         if c == 0:
             loads[1].wait()
 
-        @pl.loop(0, D // 512)
-        def _(j):
-            at = take(j * 512, 512)
+        for at in tiles(D):
             product = jnp.dot(active[c], w_out[:, at], preferred_element_type=F32)
             fwd_own[c, :, at] = product[0 : 4 * part]
             fwd_part[c, :, at] = product.astype(BF16)
@@ -222,7 +238,7 @@
         head[c].append(send(mine, mine, vocab_peer(0, 0, 1)))
 
     loads[2].wait()
-    lane = lax.broadcasted_iota(jnp.int32, (1, 512), 1)
+    lane = lax.broadcasted_iota(jnp.int32, (1, TILE), 1)
     exchange = []
     top = []
     for c in chunks:
@@ -234,31 +250,23 @@
         for copy in across:
             copy.wait_recv()
 
-        def logits_tile(j, best):
-            at = take(j * 512, 512)
+        best = jnp.full((rows, 128), -1e30, F32)
+        for at in tiles(padded_vocab):
             tile = lax.dot_general(head_all[c], embed[at, :], NT, preferred_element_type=F32)
-            here = lane + j * 512
+            here = lane + at.start
             live = jnp.logical_and(here < local_vocab, here + vocab * local_vocab < VOCAB)
             tile = jnp.where(live, tile * factor, -1e30)
             logits[c, :, at] = tile
-            for k in range(4):
+            for k in range(TILE // 128):
                 best = jnp.maximum(best, tile[:, k * 128 : (k + 1) * 128])
-            return best
-
-        best = lax.fori_loop(
-            0, padded_vocab // 512, logits_tile, jnp.full((rows, 128), -1e30, F32)
-        )
         local_top = jnp.max(best, axis=1, keepdims=True)
 
-        def exp_tile(j, acc):
-            at = take(j * 512, 512)
+        acc = jnp.zeros((rows, 128), F32)
+        for at in tiles(padded_vocab):
             tile = jnp.exp(logits[c, :, at] - local_top)
             logits[c, :, at] = tile
-            for k in range(4):
+            for k in range(TILE // 128):
                 acc = acc + tile[:, k * 128 : (k + 1) * 128]
-            return acc
-
-        acc = lax.fori_loop(0, padded_vocab // 512, exp_tile, jnp.zeros((rows, 128), F32))
         local_sum = jnp.sum(acc, axis=1, keepdims=True)
         halves = rows // 128
         stats[c] = jnp.zeros((8, 128), F32)
@@ -286,28 +294,28 @@
         )
         wanted = label[c].astype(jnp.int32) - vocab * local_vocab
 
-        @pl.loop(0, padded_vocab // 512)
-        def _(j):
-            at = take(j * 512, 512)
-            onehot = (lane + j * 512 == wanted).astype(F32)
+        for at in tiles(padded_vocab):
+            onehot = (lane + at.start == wanted).astype(F32)
             grads[c, :, at] = (weight[c] * (logits[c, :, at] * ratio - onehot)).astype(BF16)
 
-        @pl.loop(0, D // 512)
-        def _(j):
-            at = take(j * 512, 512)
+        half = rows // 2
+        across = []
+        for at in tiles(D):
             product = jnp.dot(grads[c], embed[:, at], preferred_element_type=F32) * factor
             head_part[c, :, at] = product.astype(BF16)
-
-        half = rows // 2
-        head_sum.append(
-            send(
-                head_part.at[c, take((1 - core) * half, half)], head_core.at[c],
-                vocab_peer(0, 0, 1),
-            )
-        )
-
-    for c in chunks:
-        head_sum[c].wait_recv()
+            if at.stop % 512 == 0:
+                columns = pl.ds(at.stop - 512, 512)
+                across.append(
+                    send(
+                        head_part.at[c, take((1 - core) * half, half), columns],
+                        head_core.at[c, :, columns], vocab_peer(0, 0, 1),
+                    )
+                )
+        head_sum.append(across)
+
+    for c in chunks:
+        for copy in head_sum[c]:
+            copy.wait_recv()
         half = rows // 2
         total = head_part[c, take(core * half, half), :].astype(F32) + head_core[c].astype(F32)
         head_mid[c] = total.astype(BF16)
@@ -331,23 +339,21 @@
         grad_sum_ref[c] = grad_sum
         bwd_all[c, 0:part, :] = grad_sum.astype(BF16)
         bwd.append(unit_gather_start(bwd_all.at[c]))
-    bwd = [unit_gather_pass(bwd_all.at[c], *bwd[c]) for c in chunks]
+    for which in ((1, 2), (0,)):
+        for c in chunks:
+            unit_gather_pass(bwd_all.at[c], *bwd[c], which)
 
     bwd_sum = []
     for c in chunks:
-        for copy in bwd[c]:
-            copy.wait_recv()
-
-        @pl.loop(0, hidden // 512)
-        def _(j):
-            at = take(j * 512, 512)
+        for copy in bwd[c][1]:
+            copy.wait_recv()
+
+        for at in tiles(hidden):
             product = lax.dot_general(bwd_all[c], w_out[at, :], NT, preferred_element_type=F32)
             held = active[c, :, at]
             near[c, :, at] = jnp.where(held.astype(F32) > 0.0, product, 0.0).astype(BF16)
 
-        @pl.loop(0, D // 512)
-        def _(j):
-            at = take(j * 512, 512)
+        for at in tiles(D):
             product = lax.dot_general(near[c], w_in[at, :], NT, preferred_element_type=F32)
             bwd_own[c, :, at] = product[0 : 4 * part]
             bwd_part[c, :, at] = product.astype(BF16)
@@ -364,6 +370,7 @@
         out_ref[here, :] = grad_sum_ref[c] + norm_back(
             grad_normed, inputs[here], scale_in[here], gain_in_ref[...]
         )
+    assert len(started) == SENDS
     for copy in started:
         copy.wait_send()
 
@@ -405,8 +412,8 @@
         pltpu.VMEM((c, part, D), F32),
         pltpu.VMEM((c, part, D), F32),
         pltpu.SemaphoreType.DMA((3,)),
-        pltpu.SemaphoreType.DMA((160,)),
-        pltpu.SemaphoreType.DMA((160,)),
+        pltpu.SemaphoreType.DMA((SENDS,)),
+        pltpu.SemaphoreType.DMA((SENDS,)),
     ]
     vmem = pl.BlockSpec(memory_space=pltpu.VMEM)
     anywhere = pl.BlockSpec(memory_space=pl.ANY)

time: 105 us -> 102 us (0.971); the launches traced: 103 us -> 102 us
  Pallas kernels: 102 us -> 100 us
    pallas_call x1, Pallas kernels: 102 us -> 100 us  [local(): pl.pallas_call(kernel, out_shape=jax.ShapeDtypeStruct((block, D), F32), i...]
where the time goes in v2:
time: 102 us
  Pallas kernels  100 us (98%)
  local copies, waits for them, and re-layouts  1.57 us (2%)
    pallas_call x1, Pallas kernels, local(): pl.pallas_call(kernel, out_shape=jax.ShapeDtypeStruct((block, D), F32), i...  100 us

profile of v2, /device:TPU:8, one launch (start us, length us, event | category | flops | bytes accessed | tf_op | source)
XLA Modules:
  0.0 101.5 jit_solution(3034404977120113870)
XLA Ops:
  0.0 100.0 %shard_map.82 = f32[32,1024]{1,0:T(8,128)} custom-call(bf16[32,1024]{1,0:T(8,128)(2,1)} %bitcast.5, f32[1,1024]{1,0:T(1,128)} %bitcast.6, bf16[1024,2048]{1,0:T(8,128)(2,1)} %w_in_hbm.1, bf16[2048,1024]{1,0:T(8,128)(2,1)} %w_out_hbm.1, f32[1,1024]{1,0:T(1,128)} %bitcast.7, bf16[2016,1024]{1,0:T(8,128)(2,1)} %embed_hbm.1, s32[16,1,32]{2,1,0:T(1,128)} %targets_ref.1, ...), custom_call_target="tpu_custom_call" | custom-call | flops 12884901888 | bytes 12582912 | tf_op jit(solution)/shard_map/pallas_call | solution.py:420
  100.0 1.6 %copy.10 = f32[1,1,32,1024]{3,2,1,0:T(8,128)} copy(f32[1,1,32,1024]{3,2,1,0:T(8,128)} %bitcast.4) | data formatting | bytes 262144

commit v3 on v2

v3 whole, which is shorter than its diff:
```python
import functools
import math

import jax
import jax.numpy as jnp
from jax import lax
from jax.experimental import pallas as pl
from jax.experimental.pallas import tpu as pltpu
from jax.sharding import PartitionSpec as P

D = 1024
VOCAB = 32128
EPSILON = 1e-06
CHUNKS = 2
TILE = 256
SENDS = 113 * CHUNKS
ORDER = [int(c) for c in "0101010100011101010101010101010100011101"]
F32, BF16 = jnp.float32, jnp.bfloat16
MESH = pl.DeviceIdType.MESH
STEPS = (2, 1, 3)
NEAR, SIDE, FAR = 1, 2, 3
Z_STEPS = (FAR, SIDE, NEAR)
SPLIT = 256
EVERY, DIRECT, TURNED = pl.ds(0, D), pl.ds(0, SPLIT), pl.ds(SPLIT, D - SPLIT)
CHIP_STEPS = ((1, 2), (0, 2), (1, 1), (1, 3), (0, 1), (0, 3), (1, 0))
PEER_STEPS = tuple(s + (c,) for s in CHIP_STEPS for c in (0, 1)) + ((0, 0, 1),)
NT = (((1,), (1,)), ((), ()))


def norm_scale(values):
    return lax.rsqrt(jnp.mean(values * values, axis=-1, keepdims=True) + EPSILON)


def norm_back(grad_in, values, scale_rows, gain_vec):
    scaled = grad_in * gain_vec
    inner_sum = jnp.mean(scaled * values, axis=-1, keepdims=True)
    return scaled * scale_rows - values * (scale_rows * scale_rows * scale_rows) * inner_sum


def eye(rows, columns, shift=0):
    row = lax.broadcasted_iota(jnp.int32, (rows, columns), 0)
    return row + shift == lax.broadcasted_iota(jnp.int32, (rows, columns), 1)


def as_row(column):
    return jnp.sum(jnp.where(eye(128, 128), column, 0.0), axis=0, keepdims=True)


def as_column(row, mask):
    return jnp.sum(jnp.where(mask, row, 0.0), axis=1, keepdims=True)


def kernel(
    x_ref, gain_in_ref, w_in_hbm, w_out_hbm, gain_out_ref, embed_hbm, targets_ref, mask_ref,
    out_ref,
    w_in, w_out, embed, near, active, logits, grads, label, weight,
    fwd_all, fwd_part, fwd_own, fwd_x, fwd_mid, fwd_z, fwd_turn, fwd_turn_mid, fwd_turn_in,
    head_all, stats, stats_in, head_part, head_core, head_mid, head_in,
    bwd_all, bwd_part, bwd_own, bwd_x, bwd_mid, bwd_z, bwd_turn, bwd_turn_mid, bwd_turn_in,
    summed_ref, grad_sum_ref, local_sem, send_sem, recv_sem,
):
    vocab = lax.axis_index("vocab")
    unit = lax.axis_index("units")
    x_at, z_at = unit // 4, unit % 4
    core, y_at, zlo_at = vocab % 2, (vocab // 2) % 4, vocab // 8
    local_vocab = embed_hbm.shape[0]
    padded_vocab = embed.shape[0]
    block = x_ref.shape[0]
    part = block // CHUNKS
    rows = 16 * part
    hidden = w_in.shape[1]
    factor = 1.0 / math.sqrt(D)
    chunks = range(CHUNKS)

    def x_peer(dx):
        return vocab, ((x_at + dx) % 4) * 4 + z_at

    towards = 2 * zlo_at - 1

    def z_chip(z_hi, z_lo):
        return z_lo * 8 + y_at * 2 + core, x_at * 4 + z_hi % 4

    def z_peer(k):
        if k == SIDE:
            return z_chip(z_at + 4 - towards, zlo_at)
        return z_chip(z_at + (4 + towards if k == NEAR else 2), 1 - zlo_at)

    def z_source(k):
        return z_chip(z_at + 4 + towards, zlo_at) if k == SIDE else z_peer(k)

    def vocab_peer(dzlo, dy, dcore):
        return ((zlo_at + dzlo) % 2) * 8 + ((y_at + dy) % 4) * 2 + (core + dcore) % 2, unit

    def chip_slot(dzlo, dy):
        return ((zlo_at + dzlo) % 2) * 4 + (y_at + dy) % 4

    def tiles(size):
        return [slice(start, start + TILE) for start in range(0, size, TILE)]

    def take(start, size):
        return pl.ds(pl.multiple_of(start, size), size)

    used = [0]
    started = []

    def send(src, dst, peer):
        k = used[0]
        used[0] += 1
        copy = pltpu.make_async_remote_copy(
            src_ref=src, dst_ref=dst, send_sem=send_sem.at[k], recv_sem=recv_sem.at[k],
            device_id=peer, device_id_type=MESH,
        )
        copy.start()
        started.append(copy)
        return copy

    loads = [
        pltpu.make_async_copy(w_in_hbm, w_in, local_sem.at[0]),
        pltpu.make_async_copy(w_out_hbm, w_out, local_sem.at[1]),
        pltpu.make_async_copy(embed_hbm, embed.at[pl.ds(0, local_vocab)], local_sem.at[2]),
    ]
    for load in loads:
        load.start()

    barrier = pltpu.get_barrier_semaphore()
    greet = [x_peer(d) for d in STEPS] + [z_peer(k) for k in Z_STEPS] + [z_source(SIDE)]
    greet += [vocab_peer(*s) for s in PEER_STEPS]
    for peer in greet:
        pl.semaphore_signal(barrier, inc=1, device_id=peer, device_id_type=MESH)

    inputs = x_ref[...].astype(F32)
    scale_in = norm_scale(inputs)
    normed = (inputs * scale_in * gain_in_ref[...]).astype(BF16)
    for c in chunks:
        fwd_all[c, 0:part, :] = normed[c * part : (c + 1) * part]
    embed[local_vocab:, :] = jnp.zeros((padded_vocab - local_vocab, D), BF16)
    pl.semaphore_wait(barrier, len(greet))

    my_slot = core * 8 + chip_slot(0, 0)

    def unit_gather(buf):
        def block(dx, k, columns=EVERY):
            return buf.at[pl.ds((dx * 4 + k) * part, part), columns]

        along_z = [send(block(0, 0), block(0, k), z_peer(k)) for k in Z_STEPS]
        along_x = [send(block(0, 0), block(4 - d, 0), x_peer(d)) for d in STEPS]
        across = along_x[:1]
        landed = along_x[1:]
        for k, copy in reversed(list(zip(Z_STEPS, along_z))):
            if k != SIDE:
                yield
            copy.wait_recv()
            for d in STEPS:
                columns = DIRECT if d == 2 else EVERY
                landed.append(send(block(0, k, columns), block(4 - d, k, columns), x_peer(d)))
            if k == NEAR:
                across[0].wait_recv()
                landed += [
                    send(block(2, 0, TURNED), block(2, m, TURNED), z_peer(m)) for m in Z_STEPS
                ]
        yield
        for copy in landed:
            copy.wait_recv()

    def unit_sum(partial, own, landing, mid, landing_z, turn, turn_mid, turn_in):
        def block(dx, k, columns=EVERY):
            return partial.at[pl.ds((dx * 4 + k) * part, part), columns]

        def rows_of(k):
            return slice(k * part, (k + 1) * part)

        turning = [send(block(2, k, TURNED), turn.at[k - 1], z_source(k)) for k in Z_STEPS]
        along_x = {}
        for k in Z_STEPS + (0,):
            along_x[k] = []
            for d in STEPS:
                columns = DIRECT if d == 2 else EVERY
                to = landing.at[d - 1, pl.ds(k * part, part), columns]
                along_x[k].append(send(block(d, k, columns), to, x_peer(d)))
        along_z = []
        for k in Z_STEPS + (0,):
            if k != NEAR:
                yield
            if k == SIDE:
                for copy in turning:
                    copy.wait_recv()
                total = partial[8 * part : 9 * part, SPLIT:].astype(F32)
                for m in range(3):
                    total = total + turn[m].astype(F32)
                turn_mid[...] = total.astype(BF16)
                turned = send(turn_mid, turn_in, x_peer(2))
            for copy in along_x[k]:
                copy.wait_recv()
            at = rows_of(k)
            total = own[at, :] + landing[0, at, :].astype(F32) + landing[2, at, :].astype(F32)
            direct = total[:, :SPLIT] + landing[1, at, :SPLIT].astype(F32)
            if k:
                mid[at, :SPLIT] = direct.astype(BF16)
                mid[at, SPLIT:] = total[:, SPLIT:].astype(BF16)
                along_z.append(send(mid.at[pl.ds(k * part, part)], landing_z.at[k - 1], z_source(k)))
        yield
        for copy in along_z + [turned]:
            copy.wait_recv()
        total = jnp.concatenate([direct, total[:, SPLIT:] + turn_in[...].astype(F32)], axis=1)
        for m in range(3):
            total = total + landing_z[m].astype(F32)
        return total

    lane = lax.broadcasted_iota(jnp.int32, (1, TILE), 1)
    half = rows // 2

    def chain(c):
        here = slice(c * part, (c + 1) * part)
        gather = unit_gather(fwd_all.at[c])
        next(gather)
        yield

        pick = eye(part, block, c * part)
        for slot in range(16):
            owner = ((slot // 4) % 2) * 8 + (slot % 4) * 2 + slot // 8
            at = slice(slot * part, (slot + 1) * part)
            label[c, at, :] = as_column(targets_ref[owner].astype(F32), pick)
            weight[c, at, :] = as_column(mask_ref[owner].astype(F32), pick)
        yield from gather

        if c == 0:
            loads[0].wait()
        for at in tiles(hidden):
            before = jnp.dot(fwd_all[c], w_in[:, at], preferred_element_type=F32)
            active[c, :, at] = jnp.maximum(before, 0.0).astype(BF16)
        if c == 0:
            loads[1].wait()
        for at in tiles(D):
            product = jnp.dot(active[c], w_out[:, at], preferred_element_type=F32)
            fwd_own[c, :, at] = product[0 : 4 * part]
            fwd_part[c, :, at] = product.astype(BF16)
        branch = yield from unit_sum(
            fwd_part.at[c], fwd_own.at[c], fwd_x.at[c], fwd_mid.at[c], fwd_z.at[c],
            fwd_turn.at[c], fwd_turn_mid.at[c], fwd_turn_in.at[c]
        )

        summed = inputs[here] + branch
        scale_out = norm_scale(summed)
        summed_ref[c] = summed
        mine = head_all.at[c, take(my_slot * part, part)]
        mine[...] = (summed * scale_out * gain_out_ref[...]).astype(BF16)
        arrivals = [send(mine, mine, vocab_peer(*s, 0)) for s in CHIP_STEPS]
        across = [send(mine, mine, vocab_peer(0, 0, 1))]
        yield
        for copy, (dzlo, dy) in reversed(list(zip(arrivals, CHIP_STEPS))):
            copy.wait_recv()
            slot = head_all.at[c, take((core * 8 + chip_slot(-dzlo, -dy)) * part, part)]
            across.append(send(slot, slot, vocab_peer(0, 0, 1)))
        yield
        for copy in across:
            copy.wait_recv()

        if c == 0:
            loads[2].wait()
        best = jnp.full((rows, 128), -1e30, F32)
        for at in tiles(padded_vocab):
            tile = lax.dot_general(head_all[c], embed[at, :], NT, preferred_element_type=F32)
            column = lane + at.start
            live = jnp.logical_and(column < local_vocab, column + vocab * local_vocab < VOCAB)
            tile = jnp.where(live, tile * factor, -1e30)
            logits[c, :, at] = tile
            for k in range(TILE // 128):
                best = jnp.maximum(best, tile[:, k * 128 : (k + 1) * 128])
        local_top = jnp.max(best, axis=1, keepdims=True)
        acc = jnp.zeros((rows, 128), F32)
        for at in tiles(padded_vocab):
            tile = jnp.exp(logits[c, :, at] - local_top)
            logits[c, :, at] = tile
            for k in range(TILE // 128):
                acc = acc + tile[:, k * 128 : (k + 1) * 128]
        local_sum = jnp.sum(acc, axis=1, keepdims=True)
        stats[c] = jnp.zeros((8, 128), F32)
        for h in range(rows // 128):
            stats[c, h : h + 1, :] = as_row(local_top[h * 128 : (h + 1) * 128])
            stats[c, 4 + h : 5 + h, :] = as_row(local_sum[h * 128 : (h + 1) * 128])
        exchange = [
            send(stats.at[c], stats_in.at[c, k], vocab_peer(*s)) for k, s in enumerate(PEER_STEPS)
        ]
        yield
        for copy in exchange:
            copy.wait_recv()

        own_top, own_sum = stats[c, 0:4, :], stats[c, 4:8, :]
        row_top = own_top
        for k in range(len(PEER_STEPS)):
            row_top = jnp.maximum(row_top, stats_in[c, k, 0:4, :])
        row_sum = own_sum * jnp.exp(own_top - row_top)
        for k in range(len(PEER_STEPS)):
            row_sum = row_sum + stats_in[c, k, 4:8, :] * jnp.exp(stats_in[c, k, 0:4, :] - row_top)
        ratio_rows = jnp.exp(own_top - row_top) / row_sum
        ratio = jnp.concatenate(
            [as_column(ratio_rows[h : h + 1], eye(128, 128)) for h in range(rows // 128)], axis=0
        )
        wanted = label[c].astype(jnp.int32) - vocab * local_vocab
        for at in tiles(padded_vocab):
            onehot = (lane + at.start == wanted).astype(F32)
            grads[c, :, at] = (weight[c] * (logits[c, :, at] * ratio - onehot)).astype(BF16)
        across = []
        for at in tiles(D):
            product = jnp.dot(grads[c], embed[:, at], preferred_element_type=F32) * factor
            head_part[c, :, at] = product.astype(BF16)
            if at.stop % 512 == 0:
                columns = pl.ds(at.stop - 512, 512)
                across.append(
                    send(
                        head_part.at[c, take((1 - core) * half, half), columns],
                        head_core.at[c, :, columns], vocab_peer(0, 0, 1),
                    )
                )
        yield
        for copy in across:
            copy.wait_recv()

        total = head_part[c, take(core * half, half), :].astype(F32) + head_core[c].astype(F32)
        head_mid[c] = total.astype(BF16)
        arrivals = [
            send(
                head_mid.at[c, take(chip_slot(*s) * part, part)], head_in.at[c, k],
                vocab_peer(*s, 0),
            )
            for k, s in enumerate(CHIP_STEPS)
        ]
        yield
        for copy in arrivals:
            copy.wait_recv()

        grad_final = head_mid[c, take(chip_slot(0, 0) * part, part), :].astype(F32)
        for k in range(len(CHIP_STEPS)):
            grad_final = grad_final + head_in[c, k].astype(F32)
        summed = summed_ref[c]
        grad_sum = norm_back(grad_final, summed, norm_scale(summed), gain_out_ref[...])
        grad_sum_ref[c] = grad_sum
        bwd_all[c, 0:part, :] = grad_sum.astype(BF16)
        yield from unit_gather(bwd_all.at[c])

        for at in tiles(hidden):
            product = lax.dot_general(bwd_all[c], w_out[at, :], NT, preferred_element_type=F32)
            held = active[c, :, at].astype(F32)
            near[c, :, at] = jnp.where(held > 0.0, product, 0.0).astype(BF16)
        for at in tiles(D):
            product = lax.dot_general(near[c], w_in[at, :], NT, preferred_element_type=F32)
            bwd_own[c, :, at] = product[0 : 4 * part]
            bwd_part[c, :, at] = product.astype(BF16)
        grad_normed = yield from unit_sum(
            bwd_part.at[c], bwd_own.at[c], bwd_x.at[c], bwd_mid.at[c], bwd_z.at[c],
            bwd_turn.at[c], bwd_turn_mid.at[c], bwd_turn_in.at[c]
        )
        out_ref[here, :] = grad_sum_ref[c] + norm_back(
            grad_normed, inputs[here], scale_in[here], gain_in_ref[...]
        )

    chains = [chain(c) for c in chunks]
    for c in ORDER:
        next(chains[c], None)
    assert len(started) == SENDS
    for copy in started:
        copy.wait_send()


def local(x_rows, gain_in, w_in, w_out, gain_out, embed, targets, row_mask):
    block = x_rows.shape[2]
    part = block // CHUNKS
    rows = 16 * part
    hidden = w_in.shape[1]
    padded_vocab = (embed.shape[0] + 511) // 512 * 512
    c = CHUNKS
    unit_sum = [
        pltpu.VMEM((c, rows, D), BF16),
        pltpu.VMEM((c, rows, D), BF16),
        pltpu.VMEM((c, 4 * part, D), F32),
        pltpu.VMEM((c, 3, 4 * part, D), BF16),
        pltpu.VMEM((c, 4 * part, D), BF16),
        pltpu.VMEM((c, 3, part, D), BF16),
        pltpu.VMEM((c, 3, part, D - SPLIT), BF16),
        pltpu.VMEM((c, part, D - SPLIT), BF16),
        pltpu.VMEM((c, part, D - SPLIT), BF16),
    ]
    scratch = [
        pltpu.VMEM(w_in.shape, BF16),
        pltpu.VMEM(w_out.shape, BF16),
        pltpu.VMEM((padded_vocab, D), BF16),
        pltpu.VMEM((c, rows, hidden), BF16),
        pltpu.VMEM((c, rows, hidden), BF16),
        pltpu.VMEM((c, rows, padded_vocab), F32),
        pltpu.VMEM((c, rows, padded_vocab), BF16),
        pltpu.VMEM((c, rows, 1), F32),
        pltpu.VMEM((c, rows, 1), F32),
        *unit_sum,
        pltpu.VMEM((c, rows, D), BF16),
        pltpu.VMEM((c, 8, 128), F32),
        pltpu.VMEM((c, 15, 8, 128), F32),
        pltpu.VMEM((c, rows, D), BF16),
        pltpu.VMEM((c, rows // 2, D), BF16),
        pltpu.VMEM((c, rows // 2, D), BF16),
        pltpu.VMEM((c, 7, part, D), BF16),
        *unit_sum,
        pltpu.VMEM((c, part, D), F32),
        pltpu.VMEM((c, part, D), F32),
        pltpu.SemaphoreType.DMA((3,)),
        pltpu.SemaphoreType.DMA((SENDS,)),
        pltpu.SemaphoreType.DMA((SENDS,)),
    ]
    vmem = pl.BlockSpec(memory_space=pltpu.VMEM)
    anywhere = pl.BlockSpec(memory_space=pl.ANY)
    result = pl.pallas_call(
        kernel,
        out_shape=jax.ShapeDtypeStruct((block, D), F32),
        in_specs=[vmem, vmem, anywhere, anywhere, vmem, anywhere, vmem, vmem],
        out_specs=vmem,
        scratch_shapes=scratch,
        compiler_params=pltpu.CompilerParams(
            collective_id=0, has_side_effects=True, vmem_limit_bytes=56 * 1024 * 1024
        ),
        cost_estimate=pl.CostEstimate(
            flops=12 * 512 * D * hidden, bytes_accessed=6 * hidden * D, transcendentals=0
        ),
    )(
        x_rows.reshape(block, D), gain_in.reshape(1, D), w_in, w_out, gain_out.reshape(1, D), embed,
        targets, row_mask,
    )
    return result.reshape(1, 1, block, D)


def solution(mesh):
    in_specs = (
        P("vocab", "units", None, None),
        P(),
        P(None, "units"),
        P("units", None),
        P(),
        P("vocab", None),
        P(None, "units", None),
        P(None, "units", None),
    )
    out_specs = P("vocab", "units", None, None)
    return jax.shard_map(local, mesh=mesh, in_specs=in_specs, out_specs=out_specs, check_vma=False)
```

time: 102 us -> 93.2 us (0.914); the launches traced: 102 us -> 91.6 us
  Pallas kernels: 100 us -> 90.1 us
    pallas_call x1, Pallas kernels: 100 us -> 90.1 us  [local(): pl.pallas_call(kernel, out_shape=jax.ShapeDtypeStruct((block, D), F32), i...]
where the time goes in v3:
time: 93.2 us; the launch traced here: 91.6 us
  Pallas kernels  90.1 us (97%)
  local copies, waits for them, and re-layouts  1.57 us (2%)
    pallas_call x1, Pallas kernels, local(): pl.pallas_call(kernel, out_shape=jax.ShapeDtypeStruct((block, D), F32), i...  90.1 us

profile of v3, /device:TPU:8, one launch (start us, length us, event | category | flops | bytes accessed | tf_op | source)
XLA Modules:
  0.0 91.6 jit_solution(4718770667441036485)
XLA Ops:
  0.0 90.1 %shard_map.82 = f32[32,1024]{1,0:T(8,128)} custom-call(bf16[32,1024]{1,0:T(8,128)(2,1)} %bitcast.5, f32[1,1024]{1,0:T(1,128)} %bitcast.6, bf16[1024,2048]{1,0:T(8,128)(2,1)} %w_in_hbm.1, bf16[2048,1024]{1,0:T(8,128)(2,1)} %w_out_hbm.1, f32[1,1024]{1,0:T(1,128)} %bitcast.7, bf16[2016,1024]{1,0:T(8,128)(2,1)} %embed_hbm.1, s32[16,1,32]{2,1,0:T(1,128)} %targets_ref.1, ...), custom_call_target="tpu_custom_call" | custom-call | flops 12884901888 | bytes 12582912 | tf_op jit(solution)/shard_map/pallas_call | solution.py:410
  90.1 1.6 %copy.10 = f32[1,1,32,1024]{3,2,1,0:T(8,128)} copy(f32[1,1,32,1024]{3,2,1,0:T(8,128)} %bitcast.4) | data formatting | bytes 262144

commit v4 on v3

--- a/solution.py
+++ b/solution.py
@@ -14,7 +14,7 @@
 CHUNKS = 2
 TILE = 256
 SENDS = 113 * CHUNKS
-ORDER = [int(c) for c in "0101010100011101010101010101010100011101"]
+ORDER = [int(c) for c in "0100110100011101010101010100110100011101"]
 F32, BF16 = jnp.float32, jnp.bfloat16
 MESH = pl.DeviceIdType.MESH
 STEPS = (2, 1, 3)

time: 93.2 us -> 89.5 us (0.960)
  Pallas kernels: 90.1 us -> 87.1 us
    pallas_call x1, Pallas kernels: 90.1 us -> 87.1 us  [local(): pl.pallas_call(kernel, out_shape=jax.ShapeDtypeStruct((block, D), F32), i...]
where the time goes in v4:
time: 89.5 us; the launch traced here: 88.7 us
  Pallas kernels  87.1 us (97%)
  local copies, waits for them, and re-layouts  1.57 us (2%)
    pallas_call x1, Pallas kernels, local(): pl.pallas_call(kernel, out_shape=jax.ShapeDtypeStruct((block, D), F32), i...  87.1 us

profile of v4, /device:TPU:8, one launch (start us, length us, event | category | flops | bytes accessed | tf_op | source)
XLA Modules:
  0.0 88.7 jit_solution(14029994024250889957)
XLA Ops:
  0.0 87.1 %shard_map.82 = f32[32,1024]{1,0:T(8,128)} custom-call(bf16[32,1024]{1,0:T(8,128)(2,1)} %bitcast.5, f32[1,1024]{1,0:T(1,128)} %bitcast.6, bf16[1024,2048]{1,0:T(8,128)(2,1)} %w_in_hbm.1, bf16[2048,1024]{1,0:T(8,128)(2,1)} %w_out_hbm.1, f32[1,1024]{1,0:T(1,128)} %bitcast.7, bf16[2016,1024]{1,0:T(8,128)(2,1)} %embed_hbm.1, s32[16,1,32]{2,1,0:T(1,128)} %targets_ref.1, ...), custom_call_target="tpu_custom_call" | custom-call | flops 12884901888 | bytes 12582912 | tf_op jit(solution)/shard_map/pallas_call | solution.py:410
  87.2 1.6 %copy.10 = f32[1,1,32,1024]{3,2,1,0:T(8,128)} copy(f32[1,1,32,1024]{3,2,1,0:T(8,128)} %bitcast.4) | data formatting | bytes 262144

commit v5 on v4

--- a/solution.py
+++ b/solution.py
@@ -51,8 +51,9 @@
 
 
 def kernel(
-    x_ref, gain_in_ref, w_in_hbm, w_out_hbm, gain_out_ref, embed_hbm, targets_ref, mask_ref,
+    x_hbm, gain_in_hbm, w_in_hbm, w_out_hbm, gain_out_hbm, embed_hbm, targets_hbm, mask_hbm,
     out_ref,
+    x_ref, gain_in_ref, gain_out_ref, targets_ref, mask_ref,
     w_in, w_out, embed, near, active, logits, grads, label, weight,
     fwd_all, fwd_part, fwd_own, fwd_x, fwd_mid, fwd_z, fwd_turn, fwd_turn_mid, fwd_turn_in,
     head_all, stats, stats_in, head_part, head_core, head_mid, head_in,
@@ -114,26 +115,37 @@
         started.append(copy)
         return copy
 
+    barrier = pltpu.get_barrier_semaphore()
+    greet = [x_peer(d) for d in STEPS] + [z_peer(k) for k in Z_STEPS] + [z_source(SIDE)]
+    greet += [vocab_peer(*s) for s in PEER_STEPS]
+    for peer in greet:
+        pl.semaphore_signal(barrier, inc=1, device_id=peer, device_id_type=MESH)
+
+    small = [
+        pltpu.make_async_copy(src, dst, local_sem.at[3 + k])
+        for k, (src, dst) in enumerate(
+            (
+                (x_hbm, x_ref), (gain_in_hbm, gain_in_ref), (gain_out_hbm, gain_out_ref),
+                (targets_hbm, targets_ref), (mask_hbm, mask_ref),
+            )
+        )
+    ]
     loads = [
         pltpu.make_async_copy(w_in_hbm, w_in, local_sem.at[0]),
         pltpu.make_async_copy(w_out_hbm, w_out, local_sem.at[1]),
         pltpu.make_async_copy(embed_hbm, embed.at[pl.ds(0, local_vocab)], local_sem.at[2]),
     ]
-    for load in loads:
+    for load in small + loads:
         load.start()
-
-    barrier = pltpu.get_barrier_semaphore()
-    greet = [x_peer(d) for d in STEPS] + [z_peer(k) for k in Z_STEPS] + [z_source(SIDE)]
-    greet += [vocab_peer(*s) for s in PEER_STEPS]
-    for peer in greet:
-        pl.semaphore_signal(barrier, inc=1, device_id=peer, device_id_type=MESH)
+    embed[local_vocab:, :] = jnp.zeros((padded_vocab - local_vocab, D), BF16)
+    for load in small:
+        load.wait()
 
     inputs = x_ref[...].astype(F32)
     scale_in = norm_scale(inputs)
     normed = (inputs * scale_in * gain_in_ref[...]).astype(BF16)
     for c in chunks:
         fwd_all[c, 0:part, :] = normed[c * part : (c + 1) * part]
-    embed[local_vocab:, :] = jnp.zeros((padded_vocab - local_vocab, D), BF16)
     pl.semaphore_wait(barrier, len(greet))
 
     my_slot = core * 8 + chip_slot(0, 0)
@@ -153,7 +165,7 @@
             for d in STEPS:
                 columns = DIRECT if d == 2 else EVERY
                 landed.append(send(block(0, k, columns), block(4 - d, k, columns), x_peer(d)))
-            if k == NEAR:
+            if k == FAR:
                 across[0].wait_recv()
                 landed += [
                     send(block(2, 0, TURNED), block(2, m, TURNED), z_peer(m)) for m in Z_STEPS
@@ -381,6 +393,11 @@
         pltpu.VMEM((c, part, D - SPLIT), BF16),
     ]
     scratch = [
+        pltpu.VMEM((block, D), BF16),
+        pltpu.VMEM((1, D), F32),
+        pltpu.VMEM((1, D), F32),
+        pltpu.VMEM(targets.shape, jnp.int32),
+        pltpu.VMEM(row_mask.shape, jnp.int32),
         pltpu.VMEM(w_in.shape, BF16),
         pltpu.VMEM(w_out.shape, BF16),
         pltpu.VMEM((padded_vocab, D), BF16),
@@ -401,7 +418,7 @@
         *unit_sum,
         pltpu.VMEM((c, part, D), F32),
         pltpu.VMEM((c, part, D), F32),
-        pltpu.SemaphoreType.DMA((3,)),
+        pltpu.SemaphoreType.DMA((8,)),
         pltpu.SemaphoreType.DMA((SENDS,)),
         pltpu.SemaphoreType.DMA((SENDS,)),
     ]
@@ -410,7 +427,7 @@
     result = pl.pallas_call(
         kernel,
         out_shape=jax.ShapeDtypeStruct((block, D), F32),
-        in_specs=[vmem, vmem, anywhere, anywhere, vmem, anywhere, vmem, vmem],
+        in_specs=[anywhere] * 8,
         out_specs=vmem,
         scratch_shapes=scratch,
         compiler_params=pltpu.CompilerParams(

time: 89.5 us -> 88.3 us (0.987)
  Pallas kernels: 87.1 us -> 85.3 us
    pallas_call x1, Pallas kernels: 87.1 us -> 85.3 us  [local(): pl.pallas_call(kernel, out_shape=jax.ShapeDtypeStruct((block, D), F32), i...]
where the time goes in v5:
time: 88.3 us; the launch traced here: 86.9 us
  Pallas kernels  85.3 us (97%)
  local copies, waits for them, and re-layouts  1.57 us (2%)
    pallas_call x1, Pallas kernels, local(): pl.pallas_call(kernel, out_shape=jax.ShapeDtypeStruct((block, D), F32), i...  85.3 us

profile of v5, /device:TPU:8, one launch (start us, length us, event | category | flops | bytes accessed | tf_op | source)
XLA Modules:
  0.0 86.9 jit_solution(7730763876640730891)
XLA Ops:
  0.0 85.3 %shard_map.82 = f32[32,1024]{1,0:T(8,128)} custom-call(bf16[32,1024]{1,0:T(8,128)(2,1)} %bitcast.5, f32[1,1024]{1,0:T(1,128)} %bitcast.6, bf16[1024,2048]{1,0:T(8,128)(2,1)} %w_in_hbm.1, bf16[2048,1024]{1,0:T(8,128)(2,1)} %w_out_hbm.1, f32[1,1024]{1,0:T(1,128)} %bitcast.7, bf16[2016,1024]{1,0:T(8,128)(2,1)} %embed_hbm.1, s32[16,1,32]{2,1,0:T(1,128)} %targets_hbm.1, ...), custom_call_target="tpu_custom_call" | custom-call | flops 12884901888 | bytes 12582912 | tf_op jit(solution)/shard_map/pallas_call | solution.py:427
  85.3 1.6 %copy.10 = f32[1,1,32,1024]{3,2,1,0:T(8,128)} copy(f32[1,1,32,1024]{3,2,1,0:T(8,128)} %bitcast.4) | data formatting | bytes 262144

commit v6 on v5

--- a/solution.py
+++ b/solution.py
@@ -227,12 +227,13 @@
         next(gather)
         yield
 
-        pick = eye(part, block, c * part)
-        for slot in range(16):
-            owner = ((slot // 4) % 2) * 8 + (slot % 4) * 2 + slot // 8
-            at = slice(slot * part, (slot + 1) * part)
-            label[c, at, :] = as_column(targets_ref[owner].astype(F32), pick)
-            weight[c, at, :] = as_column(mask_ref[owner].astype(F32), pick)
+        for k in chunks if c == 0 else ():
+            pick = eye(part, block, k * part)
+            for slot in range(16):
+                owner = ((slot // 4) % 2) * 8 + (slot % 4) * 2 + slot // 8
+                at = slice(slot * part, (slot + 1) * part)
+                label[k, at, :] = as_column(targets_ref[owner].astype(F32), pick)
+                weight[k, at, :] = as_column(mask_ref[owner].astype(F32), pick)
         yield from gather
 
         if c == 0:
@@ -294,6 +295,7 @@
             send(stats.at[c], stats_in.at[c, k], vocab_peer(*s)) for k, s in enumerate(PEER_STEPS)
         ]
         yield
+        wanted = label[c].astype(jnp.int32) - vocab * local_vocab
         for copy in exchange:
             copy.wait_recv()
 
@@ -308,7 +310,6 @@
         ratio = jnp.concatenate(
             [as_column(ratio_rows[h : h + 1], eye(128, 128)) for h in range(rows // 128)], axis=0
         )
-        wanted = label[c].astype(jnp.int32) - vocab * local_vocab
         for at in tiles(padded_vocab):
             onehot = (lane + at.start == wanted).astype(F32)
             grads[c, :, at] = (weight[c] * (logits[c, :, at] * ratio - onehot)).astype(BF16)
@@ -338,14 +339,15 @@
             for k, s in enumerate(CHIP_STEPS)
         ]
         yield
+        summed = summed_ref[c]
+        scale_out = norm_scale(summed)
         for copy in arrivals:
             copy.wait_recv()
 
         grad_final = head_mid[c, take(chip_slot(0, 0) * part, part), :].astype(F32)
         for k in range(len(CHIP_STEPS)):
             grad_final = grad_final + head_in[c, k].astype(F32)
-        summed = summed_ref[c]
-        grad_sum = norm_back(grad_final, summed, norm_scale(summed), gain_out_ref[...])
+        grad_sum = norm_back(grad_final, summed, scale_out, gain_out_ref[...])
         grad_sum_ref[c] = grad_sum
         bwd_all[c, 0:part, :] = grad_sum.astype(BF16)
         yield from unit_gather(bwd_all.at[c])

time: 88.3 us -> 88.5 us (level)
  no operation moved by 1% of the time
where the time goes in v6:
time: 88.5 us; the launch traced here: 87.6 us
  Pallas kernels  86 us (97%)
  local copies, waits for them, and re-layouts  1.57 us (2%)
    pallas_call x1, Pallas kernels, local(): pl.pallas_call(kernel, out_shape=jax.ShapeDtypeStruct((block, D), F32), i...  86 us

profile of v6, /device:TPU:8, one launch (start us, length us, event | category | flops | bytes accessed | tf_op | source)
XLA Modules:
  0.0 87.6 jit_solution(14632600839342902113)
XLA Ops:
  0.0 86.0 %shard_map.82 = f32[32,1024]{1,0:T(8,128)} custom-call(bf16[32,1024]{1,0:T(8,128)(2,1)} %bitcast.5, f32[1,1024]{1,0:T(1,128)} %bitcast.6, bf16[1024,2048]{1,0:T(8,128)(2,1)} %w_in_hbm.1, bf16[2048,1024]{1,0:T(8,128)(2,1)} %w_out_hbm.1, f32[1,1024]{1,0:T(1,128)} %bitcast.7, bf16[2016,1024]{1,0:T(8,128)(2,1)} %embed_hbm.1, s32[16,1,32]{2,1,0:T(1,128)} %targets_hbm.1, ...), custom_call_target="tpu_custom_call" | custom-call | flops 12884901888 | bytes 12582912 | tf_op jit(solution)/shard_map/pallas_call | solution.py:429
  86.0 1.6 %copy.10 = f32[1,1,32,1024]{3,2,1,0:T(8,128)} copy(f32[1,1,32,1024]{3,2,1,0:T(8,128)} %bitcast.4) | data formatting | bytes 262144
